TPU v7x, 128 devices: a whole 4x4x4 slice. The times are simulated.
128 devices in a mesh: group: 4 (over y), bank: 32 (over z, x, core).
Axes of the slice: x: 4, y: 4, z: 4, core: 2. Of those that a mesh axis runs over, the one named last changes fastest.
Arguments:
- normed_layer_input: bfloat16 [128, 256, 5120], P(('group', 'bank')), may hold values from -6 to 6
- input_times_down: bfloat16 [128, 256, 16], P(('group', 'bank')), may hold values from -6 to 6
- queries: bfloat16 [128, 256, 4096], P(('group', 'bank')), may hold values from -40 to 40
- row_own_keys: bfloat16 [128, 256, 512], P(('group', 'bank')), may hold values from -8 to 8
- row_own_values: bfloat16 [128, 256, 512], P(('group', 'bank')), may hold values from -6 to 6
- output_gradient: bfloat16 [128, 256, 4096], P(('group', 'bank')), may hold values from -6 to 6
- prefix_key_bank: bfloat16 [16, 2048, 512], P(None, ('group', 'bank')), may hold values from -6 to 6
- prefix_value_bank: bfloat16 [16, 2048, 512], P(None, ('group', 'bank')), may hold values from -6 to 6
- live_prefix_length: int32 [16], replicated, may hold values from 512 to 2048, as said below
- tenant: int32 [128], replicated, may hold values from 0 to 15
- tenant_bank_slot: int32 [16], replicated, may hold values from 0 to 15, each once
- tenant_adapter_slot: int32 [16], replicated, may hold values from 0 to 15, each once
- query_up_adapters: bfloat16 [16, 16, 4096], replicated, may hold values from -1.5 to 1.5
Outputs:
- query_grad: bfloat16 [128, 256, 4096], P(('group', 'bank'))
- down_grad: float32 [16, 16, 5120], P('group', None, 'bank')
- up_grad: float32 [16, 16, 4096], P('group', None, 'bank')
Inputs may be any that keep to these rules, and one draw needn't show every extreme that they name: `live_prefix_length`: some tenant's whole prefix is live.
All inputs are finite; a program needn't handle non-finite values.
Results may differ from a plain program's by a relative error of at most 0.0064.
Values may be sent and summed in bfloat16 or wider, within the bound.
No kernel may reach another device: no remote copies, remote signals or barrier semaphores. Data moves between devices by JAX's collectives and lax.ppermute only.
A program may use at most 192 MiB of HBM per device.

v0:
```python
import math

import jax
import jax.numpy as jnp
from jax import lax
from jax.experimental import pallas as pl
from jax.experimental.pallas import tpu as pltpu
from jax.sharding import PartitionSpec as P

SEQ = 256
PREFIX = 2048
HEAD = 128
KV_HEADS = 4
GROUP = 8
RANK = 16
KEY_BLOCK = 256
BLOCKS = PREFIX // KEY_BLOCK
ALL_KEYS = PREFIX + SEQ
LEAST_LIVE = 512
SLOTS = 16
MASKED = -1e30
SCALE = HEAD**-0.5
SCALE2 = SCALE * math.log2(math.e)
ADAPTER_SCALE = 2.0
ROWS_AT_ONCE = 16
UP = 128
DOWN = 160
TERM = 384


def dot(a, b, a_dim, b_dim):
    return lax.dot_general(
        a, b, (((a_dim,), (b_dim,)), ((), ())), preferred_element_type=jnp.float32
    )


def attention_kernel(
    own, tenant, lengths, adapter_slot,
    q_ref, grad_ref, key_ref, value_ref, own_key_ref, own_value_ref, adapter_ref, mid_in_ref, x_ref,
    dq_ref, t0_ref, t1_ref, t2_ref, t3_ref,
    scores, probs, score_grad, bias, mid_sum, down,
):
    g = pl.program_id(0)
    length = lengths[tenant[own[0]]]
    position = lax.broadcasted_iota(jnp.int32, bias.shape, 1)
    bias[...] = jnp.where(position < length, 0.0, MASKED)

    def block(prefix_ref, own_ref, j):
        return prefix_ref[j * KEY_BLOCK : (j + 1) * KEY_BLOCK, :] if j < BLOCKS else own_ref[...]

    def head(h, carry):
        columns = pl.ds(pl.multiple_of(h * HEAD, HEAD), HEAD)
        q = q_ref[:, columns]
        grad = grad_ref[:, columns]
        for j in range(BLOCKS + 1):
            s = dot(q, block(key_ref, own_key_ref, j), 1, 1)
            if j == BLOCKS:
                row = lax.broadcasted_iota(jnp.int32, (SEQ, SEQ), 0)
                column = lax.broadcasted_iota(jnp.int32, (SEQ, SEQ), 1)
                s = jnp.where(column <= row, s, MASKED)
            elif (j + 1) * KEY_BLOCK > LEAST_LIVE:
                s = s + bias[0:1, j * KEY_BLOCK : (j + 1) * KEY_BLOCK]
            scores[:, j * KEY_BLOCK : (j + 1) * KEY_BLOCK] = s
        for j in range(BLOCKS + 1):
            probs[:, j * KEY_BLOCK : (j + 1) * KEY_BLOCK] = dot(
                grad, block(value_ref, own_value_ref, j), 1, 1
            )
        for r in range(0, SEQ, ROWS_AT_ONCE):
            rows = slice(r, r + ROWS_AT_ONCE)
            s = scores[rows, :]
            top = jnp.max(s, axis=-1, keepdims=True)
            e = jnp.exp2(s * SCALE2 - top * SCALE2)
            weights = e * (1.0 / jnp.sum(e, axis=-1, keepdims=True))
            weights_low = weights.astype(jnp.bfloat16).astype(jnp.float32)
            prob_grad = probs[rows, :]
            delta = jnp.sum(weights_low * prob_grad, axis=-1, keepdims=True)
            score_grad[rows, :] = (weights * (prob_grad - delta)).astype(jnp.bfloat16)
        total = dot(score_grad[:, :PREFIX], key_ref[...], 1, 0)
        total += dot(score_grad[:, PREFIX:], own_key_ref[...], 1, 0)
        dq_ref[:, columns] = (total * SCALE).astype(jnp.bfloat16)
        return carry

    lax.fori_loop(0, GROUP, head, 0)

    @pl.when(g == 0)
    def _():
        mid_sum[...] = jnp.zeros_like(mid_sum)

    dq = dq_ref[...]
    mid_sum[...] += dot(dq, adapter_ref[0], 1, 1)
    up = (ADAPTER_SCALE * dot(mid_in_ref[...], dq, 0, 0)).astype(jnp.bfloat16)

    bank = lax.rem(own[0], 32)
    my_z, my_x, my_core = bank // 8, lax.rem(bank // 2, 4), lax.rem(bank, 2)
    terms = (t0_ref, t1_ref, t2_ref, t3_ref)

    def place(b, write):
        z, x, core = b // 8, lax.rem(b // 2, 4), lax.rem(b, 2)
        far_z, far_x = lax.rem(z - my_z + 4, 4), lax.rem(x - my_x + 4, 4)
        far_core = jnp.where(core == my_core, 0, 1)
        at = far_z * 2 + far_core
        for k in range(4):

            @pl.when(far_x == k)
            def _():
                write(terms[k], at)

    for i in range(GROUP):
        def write_up(ref, at, i=i):
            ref[at, :, 0:UP] = up[:, i * UP : (i + 1) * UP]

        place(g * GROUP + i, write_up)

    @pl.when(g == KV_HEADS - 1)
    def _():
        mid = mid_sum[...].astype(jnp.bfloat16)
        down[...] = ADAPTER_SCALE * dot(mid, x_ref[...], 0, 0)
        for b in range(32):
            def write_down(ref, at, b=b):
                ref[at, :, UP : UP + DOWN] = down[:, b * DOWN : (b + 1) * DOWN].astype(jnp.bfloat16)
                ref[at, :, UP + DOWN :] = jnp.zeros((RANK, TERM - UP - DOWN), jnp.bfloat16)

            place(jnp.int32(b), write_down)


def attention(own, tenant, lengths, adapter_slot, q, grad, pairs, own_key, own_value, adapters, mid_in, x):
    def wide(shape):
        return pl.BlockSpec(shape, lambda g, *_: (0, g))

    def whole(shape):
        return pl.BlockSpec(shape, lambda g, *_: (0,) * len(shape))

    def adapter_at(g, own, tenant, lengths, adapter_slot):
        return (adapter_slot[tenant[own[0]]], 0, g)

    term = jax.ShapeDtypeStruct((8, RANK, TERM), jnp.bfloat16)
    return pl.pallas_call(
        attention_kernel,
        out_shape=(jax.ShapeDtypeStruct(q.shape, jnp.bfloat16),) + (term,) * 4,
        grid_spec=pltpu.PrefetchScalarGridSpec(
            num_scalar_prefetch=4,
            grid=(KV_HEADS,),
            in_specs=[
                wide((SEQ, GROUP * HEAD)),
                wide((SEQ, GROUP * HEAD)),
                wide((PREFIX, HEAD)),
                pl.BlockSpec((PREFIX, HEAD), lambda g, *_: (0, KV_HEADS + g)),
                wide((SEQ, HEAD)),
                wide((SEQ, HEAD)),
                pl.BlockSpec((1, RANK, GROUP * HEAD), adapter_at),
                whole(mid_in.shape),
                whole(x.shape),
            ],
            out_specs=(wide((SEQ, GROUP * HEAD)),) + (whole(term.shape),) * 4,
            scratch_shapes=[
                pltpu.VMEM((SEQ, ALL_KEYS), jnp.float32),
                pltpu.VMEM((SEQ, ALL_KEYS), jnp.float32),
                pltpu.VMEM((SEQ, ALL_KEYS), jnp.bfloat16),
                pltpu.VMEM((8, PREFIX), jnp.float32),
                pltpu.VMEM((SEQ, RANK), jnp.float32),
                pltpu.VMEM((RANK, x.shape[1]), jnp.float32),
            ],
        ),
        compiler_params=pltpu.CompilerParams(vmem_limit_bytes=48 << 20),
        cost_estimate=pl.CostEstimate(flops=15_000_000_000, bytes_accessed=16_000_000, transcendentals=19_000_000),
        name="attention",
    )(own, tenant, lengths, adapter_slot, q, grad, pairs, pairs, own_key, own_value, adapters, mid_in, x)


def sum_kernel(own, slots, near_ref, far_ref, a0_ref, a1_ref, a2_ref, a3_ref, total):
    total[...] = jnp.zeros_like(total)
    for half, ref in enumerate((near_ref, far_ref)):
        for i in range(16):
            slot = slots[half * 16 + i]
            total[slot] += ref[i].astype(jnp.float32)
    mine = own[0] // 32
    for k, ref in enumerate((a0_ref, a1_ref, a2_ref, a3_ref)):
        first = lax.rem(mine + k, 4) * 4
        for i in range(4):
            ref[i] = total[first + i]


def sum_terms(own, slots, near, far):
    out = jax.ShapeDtypeStruct((4, RANK, TERM), jnp.float32)
    return pl.pallas_call(
        sum_kernel,
        out_shape=(out,) * 4,
        grid_spec=pltpu.PrefetchScalarGridSpec(
            num_scalar_prefetch=2,
            grid=(1,),
            in_specs=[pl.BlockSpec((16, RANK, TERM), lambda i, *_: (0, 0, 0))] * 2,
            out_specs=[pl.BlockSpec((4, RANK, TERM), lambda i, *_: (0, 0, 0))] * 4,
            scratch_shapes=[pltpu.VMEM((SLOTS, RANK, TERM), jnp.float32)],
        ),
        name="sum_terms",
    )(own, slots, near, far)


def bank_at(z, x, core):
    return (z % 4) * 8 + (x % 4) * 2 + core


BANKS = [(z, x, c) for z in range(4) for x in range(4) for c in range(2)]


def to_x(k):
    return [(bank_at(z, x, c), bank_at(z, x + k, c)) for z, x, c in BANKS]


def to_z(k):
    return [(bank_at(z, x, c), bank_at(z + k, x, c)) for z, x, c in BANKS]


TO_CORE = [(bank_at(z, x, c), bank_at(z, x, 1 - c)) for z, x, c in BANKS]


def body(
    normed_layer_input,
    input_times_down,
    queries,
    row_own_keys,
    row_own_values,
    output_gradient,
    prefix_key_bank,
    prefix_value_bank,
    live_prefix_length,
    tenant,
    tenant_bank_slot,
    tenant_adapter_slot,
    query_up_adapters,
):
    own = lax.axis_index(("group", "bank")).astype(jnp.int32)
    own1 = own[None]
    share = jnp.concatenate([prefix_key_bank, prefix_value_bank], -1)
    send = share[tenant_bank_slot[tenant]]
    got = lax.all_to_all(send, ("group", "bank"), split_axis=0, concat_axis=0, tiled=True)
    pairs = got.reshape(PREFIX, -1)
    dq, *terms = attention(
        own1, tenant, live_prefix_length, tenant_adapter_slot, queries[0], output_gradient[0],
        pairs, row_own_keys[0], row_own_values[0], query_up_adapters, input_times_down[0],
        normed_layer_input[0],
    )
    by_x = [terms[0]] + [lax.ppermute(terms[k], "bank", to_x(k)) for k in range(1, 4)]
    held = jnp.stack([t.reshape(4, 2, RANK, TERM) for t in by_x], 1)
    by_z = [held[0]] + [lax.ppermute(held[k], "bank", to_z(k)) for k in range(1, 4)]
    held = jnp.stack(by_z, 0)
    near = held[:, :, 0].reshape(16, RANK, TERM)
    far = lax.ppermute(held[:, :, 1].reshape(16, RANK, TERM), "bank", TO_CORE)
    group, bank = own // 32, own % 32
    my_z, my_x, my_core = bank // 8, (bank // 2) % 4, bank % 2
    back = jnp.arange(4, dtype=jnp.int32)
    row_z = ((my_z - back) % 4)[None, :, None]
    row_x = ((my_x - back) % 4)[None, None, :]
    row_core = jnp.stack([my_core, 1 - my_core])[:, None, None]
    rows = (group * 32 + row_z * 8 + row_x * 2 + row_core).reshape(32)
    slots = tenant_adapter_slot[tenant[rows]]
    sums = sum_terms(own1, slots, near, far)
    for k in range(1, 4):
        part = lax.ppermute(sums[k], "group", [(i, (i + k) % 4) for i in range(4)])
        total = sums[0] + part if k == 1 else total + part
    return dq[None], total[:, :, UP : UP + DOWN], total[:, :, :UP]


def solution(mesh):
    rows = P(("group", "bank"), None, None)
    return jax.shard_map(
        body,
        mesh=mesh,
        in_specs=(rows,) * 6 + (P(None, ("group", "bank"), None),) * 2 + (P(),) * 5,
        out_specs=(rows, P("group", None, "bank"), P("group", None, "bank")),
        check_vma=False,
    )
```

profile of v0, /device:TPU:0, one launch (start us, length us, event | category | flops | bytes accessed | tf_op | source)
XLA Modules:
  0.0 183.8 jit_solution(10200316029940322614)
XLA Ops:
  0.6 2.0 %fusion.10 = (s32[1]{0:T(128)}, s32[1]{0:T(128)}, s32[1]{0:T(128)}, s32[1]{0:T(128)}, s32[1]{0:T(128)}, /*index=5*/s32[1]{0:T(128)}, s32[1]{0:T(128)}, s32[1]{0:...) fusion(s32[16]{0:T(128)} %param.23), kind=kLoop, calls=%fused_computation.52 | loop fusion | bytes 128 | tf_op jit(solution)/shard_map/gather | solution.py:235
  2.6 10.7 %fusion.6 = s32[128]{0:T(128)S(1)} fusion(s32[128]{0:T(128)} %tenant.1, s32[]{:T(128)} %bitcast.3, s32[]{:T(128)} %bitcast.4, s32[]{:T(128)} %bitcast.5, s32[]{:T(128)} %bitcast.6, s32[]{:T(128)} %bitcast.7, s32[]{:T(128)} %bitcast.8, s32[]{:T(128)} %bitcast.9, s32[]{:T(128)} %bitcast.10, s32[]{:T(128)} %bitcast.11, s32[]{:T(128)} %bitcast.12, s32[]{:T(128)} %bitcast.13, ...), kind=kLoop, calls=%fused_computation.47 | loop fusion | flops 4608 | bytes 1088 | tf_op jit(solution)/shard_map/select_n | solution.py:235
  13.3 1.1 pad_maximum_fusion
  14.4 2.8 %gather_fusion = bf16[128,16,1024]{2,1,0:T(8,128)(2,1)} fusion(bf16[16,16,1024]{2,1,0:T(8,128)(2,1)S(1)} %pad_maximum_fusion, s32[1024]{0:T(1024)S(1)} %pad_clamp_fusion.2), kind=kCustom, calls=%fused_computation | custom fusion | bytes 8389120 | tf_op jit(solution)/shard_map/gather | solution.py:235
  17.3 11.7 %all-to-all-start = ((bf16[128,16,1024]{2,1,0:T(8,128)(2,1)}), bf16[128,16,1024]{2,1,0:T(8,128)(2,1)}, u32[]{:S(2)}, u32[]{:S(2)}) async-start(bf16[128,16,1024]{2,1,0:T(8,128)(2,1)} %gather_fusion), calls=%async_computation | async-start | bytes 8388608 | tf_op jit(solution)/shard_map/all_to_all | solution.py:236
  29.6 51.9 %all-to-all-done = bf16[128,16,1024]{2,1,0:T(8,128)(2,1)} async-done(((bf16[128,16,1024]{2,1,0:T(8,128)(2,1)}), bf16[128,16,1024]{2,1,0:T(8,128)(2,1)}, u32[]{:S(2)}, u32[]{:S(2)}) %all-to-all-start) | async-done | bytes 4194336 | tf_op jit(solution)/shard_map/all_to_all | solution.py:236
  81.5 1.6 copy-done.3
  83.1 67.8 %attention.1 = (bf16[256,4096]{1,0:T(8,128)(2,1)}, bf16[8,16,384]{2,1,0:T(8,128)(2,1)S(1)}, bf16[8,16,384]{2,1,0:T(8,128)(2,1)S(1)}, bf16[8,16,384]{2,1,0:T(8,128)(2,1)S(1)}, bf16[8,16,384]{2,1,0:T(8,128)(2,1)S(1)}) custom-call(s32[1]{0:T(128)} %bitcast.own, s32[128]{0:T(128)S(1)} %copy-done, s32[16]{0:T(128)S(1)} %copy-done.6, s32[16]{0:T(128)S(1)} %copy-done.1, ...), custom_call_target="tpu_custom_call" | custom-call | flops 15000000512 | bytes 16000000 | tf_op jit(solution)/shard_map/attention/pallas_call | solution.py:137
  150.9 0.7 collective-permute-start
  151.5 1.9 %collective-permute-start.1 = (bf16[8,16,384]{2,1,0:T(8,128)(2,1)S(1)}, bf16[8,16,384]{2,1,0:T(8,128)(2,1)S(1)}, u32[]{:S(2)}, u32[]{:S(2)}) collective-permute-start(bf16[8,16,384]{2,1,0:T(8,128)(2,1)S(1)} %get-tuple-element.15), channel_id=1, source_target_pairs={{0,4},{1,5},{2,6},{3,7},{4,0},{5,1},{6,2},{7,3},{8,12},{9,13},{10,... | collective-permute-start | bytes 294920 | tf_op jit(solution)/shard_map/ppermute | solution.py:243
  153.5 0.8 collective-permute-start.2
  154.3 4.2 %collective-permute-done = bf16[8,16,384]{2,1,0:T(8,128)(2,1)S(1)} collective-permute-done((bf16[8,16,384]{2,1,0:T(8,128)(2,1)S(1)}, bf16[8,16,384]{2,1,0:T(8,128)(2,1)S(1)}, u32[]{:S(2)}, u32[]{:S(2)}) %collective-permute-start) | collective-permute-done | bytes 98336 | tf_op jit(solution)/shard_map/ppermute | solution.py:243
  159.3 1.9 %collective-permute-start.4 = (bf16[4,2,16,384]{3,2,0,1:T(8,128)(2,1)S(1)}, bf16[4,2,16,384]{3,2,0,1:T(8,128)(2,1)S(1)}, u32[]{:S(2)}, u32[]{:S(2)}) collective-permute-start(bf16[4,2,16,384]{3,2,0,1:T(8,128)(2,1)S(1)} %get-tuple-element.25), channel_id=1, source_target_pairs={{0,16},{1,17},{2,18},{3,19},{4,20},{5,21},{6,22},{7,23},{8,24},{9,... | collective-permute-start | bytes 294920 | tf_op jit(solution)/shard_map/ppermute | solution.py:245
  161.1 1.4 collective-permute-start.5
  162.5 0.7 gather_fusion.1
  163.2 2.9 %collective-permute-done.3 = bf16[4,2,16,384]{3,2,0,1:T(8,128)(2,1)S(1)} collective-permute-done((bf16[4,2,16,384]{3,2,0,1:T(8,128)(2,1)S(1)}, bf16[4,2,16,384]{3,2,0,1:T(8,128)(2,1)S(1)}, u32[]{:S(2)}, u32[]{:S(2)}) %collective-permute-start.3) | collective-permute-done | bytes 98336 | tf_op jit(solution)/shard_map/ppermute | solution.py:245
  166.1 0.9 collective-permute-done.5
  167.1 0.7 fusion.9
  167.8 1.2 gather_fusion.2
  169.9 2.6 %sum_terms.1 = (f32[4,16,384]{2,1,0:T(8,128)}, f32[4,16,384]{2,1,0:T(8,128)}, f32[4,16,384]{2,1,0:T(8,128)}, f32[4,16,384]{2,1,0:T(8,128)}) custom-call(s32[1]{0:T(128)} %bitcast.own, s32[32]{0:T(128)} %gather_fusion.2, bf16[16,16,384]{2,1,0:T(8,128)(2,1)} %bitcast.76, bf16[16,16,384]{2,1,0:T(8,128)(2,1)} %copy-done.7), custom_call_target="tpu_custom_call" | custom-call | tf_op jit(solution)/shard_map/sum_terms/pallas_call | solution.py:185
  172.6 2.3 %collective-permute-start.8 = (f32[4,16,384]{2,1,0:T(8,128)}, f32[4,16,384]{2,1,0:T(8,128)S(1)}, u32[]{:S(2)}, u32[]{:S(2)}) collective-permute-start(f32[4,16,384]{2,1,0:T(8,128)} %get-tuple-element.19), channel_id=1, source_target_pairs={{0,64},{32,96},{64,0},{96,32},{1,65},{33,97},{65,1},{97,33},{2,66}... | collective-permute-start | bytes 294920 | tf_op jit(solution)/shard_map/ppermute | solution.py:259
  174.8 1.6 collective-permute-start.9
  176.5 4.6 %collective-permute-done.7 = f32[4,16,384]{2,1,0:T(8,128)S(1)} collective-permute-done((f32[4,16,384]{2,1,0:T(8,128)}, f32[4,16,384]{2,1,0:T(8,128)S(1)}, u32[]{:S(2)}, u32[]{:S(2)}) %collective-permute-start.7) | collective-permute-done | bytes 98336 | tf_op jit(solution)/shard_map/ppermute | solution.py:259
  181.7 0.9 add_add_fusion
  (42 shorter events, 4.1 us)
Async XLA Ops:
  17.3 11.8 %copy-start.8 = (bf16[1,256,16]{1,2,0:T(8,128)(2,1)S(1)}, bf16[1,256,16]{1,2,0:T(8,128)(2,1)}, u32[]{:S(2)}) copy-start(bf16[1,256,16]{1,2,0:T(8,128)(2,1)} %param.14) | copy-start | bytes 24580
  17.3 64.2 %copy-start = (s32[128]{0:T(128)S(1)}, s32[128]{0:T(128)}, u32[]{:S(2)}) copy-start(s32[128]{0:T(128)} %tenant.1) | copy-start | bytes 1540
  17.3 64.2 %copy-start.1 = (s32[16]{0:T(128)S(1)}, s32[16]{0:T(128)}, u32[]{:S(2)}) copy-start(s32[16]{0:T(128)} %adapter_slot.1) | copy-start | bytes 196
  17.3 64.2 %copy-start.2 = (bf16[1,256,4096]{2,1,0:T(8,128)(2,1)S(1)}, bf16[1,256,4096]{2,1,0:T(8,128)(2,1)}, u32[]{:S(2)}) copy-start(bf16[1,256,4096]{2,1,0:T(8,128)(2,1)} %param.15) | copy-start | bytes 6291460
  17.3 64.2 %copy-start.4 = (bf16[1,256,512]{2,1,0:T(8,128)(2,1)S(1)}, bf16[1,256,512]{2,1,0:T(8,128)(2,1)}, u32[]{:S(2)}) copy-start(bf16[1,256,512]{2,1,0:T(8,128)(2,1)} %param.16) | copy-start | bytes 786436
  17.3 64.2 %copy-start.5 = (bf16[1,256,512]{2,1,0:T(8,128)(2,1)S(1)}, bf16[1,256,512]{2,1,0:T(8,128)(2,1)}, u32[]{:S(2)}) copy-start(bf16[1,256,512]{2,1,0:T(8,128)(2,1)} %param.17) | copy-start | bytes 786436
  17.3 64.2 %copy-start.6 = (s32[16]{0:T(128)S(1)}, s32[16]{0:T(128)}, u32[]{:S(2)}) copy-start(s32[16]{0:T(128)} %lengths.1) | copy-start | bytes 196
  17.3 64.1 %all-to-all-start = ((bf16[128,16,1024]{2,1,0:T(8,128)(2,1)}), bf16[128,16,1024]{2,1,0:T(8,128)(2,1)}, u32[]{:S(2)}, u32[]{:S(2)}) async-start(bf16[128,16,1024]{2,1,0:T(8,128)(2,1)} %gather_fusion), calls=%async_computation | async-start | bytes 8388608 | tf_op jit(solution)/shard_map/all_to_all | solution.py:236
  81.5 1.6 copy-start.3
  150.9 7.6 %collective-permute-start = (bf16[8,16,384]{2,1,0:T(8,128)(2,1)S(1)}, bf16[8,16,384]{2,1,0:T(8,128)(2,1)S(1)}, u32[]{:S(2)}, u32[]{:S(2)}) collective-permute-start(bf16[8,16,384]{2,1,0:T(8,128)(2,1)S(1)} %get-tuple-element.14), channel_id=1, source_target_pairs={{0,2},{1,3},{2,4},{3,5},{4,6},{5,7},{6,0},{7,1},{8,10},{9,11},{10,... | collective-permute-start | bytes 294920 | tf_op jit(solution)/shard_map/ppermute | solution.py:243
  151.5 6.9 %collective-permute-start.1 = (bf16[8,16,384]{2,1,0:T(8,128)(2,1)S(1)}, bf16[8,16,384]{2,1,0:T(8,128)(2,1)S(1)}, u32[]{:S(2)}, u32[]{:S(2)}) collective-permute-start(bf16[8,16,384]{2,1,0:T(8,128)(2,1)S(1)} %get-tuple-element.15), channel_id=1, source_target_pairs={{0,4},{1,5},{2,6},{3,7},{4,0},{5,1},{6,2},{7,3},{8,12},{9,13},{10,... | collective-permute-start | bytes 294920 | tf_op jit(solution)/shard_map/ppermute | solution.py:243
  153.5 5.6 %collective-permute-start.2 = (bf16[8,16,384]{2,1,0:T(8,128)(2,1)S(1)}, bf16[8,16,384]{2,1,0:T(8,128)(2,1)S(1)}, u32[]{:S(2)}, u32[]{:S(2)}) collective-permute-start(bf16[8,16,384]{2,1,0:T(8,128)(2,1)S(1)} %get-tuple-element.16), channel_id=1, source_target_pairs={{0,6},{1,7},{2,0},{3,1},{4,2},{5,3},{6,4},{7,5},{8,14},{9,15},{10,... | collective-permute-start | bytes 294920 | tf_op jit(solution)/shard_map/ppermute | solution.py:243
  159.2 7.0 %collective-permute-start.3 = (bf16[4,2,16,384]{3,2,0,1:T(8,128)(2,1)S(1)}, bf16[4,2,16,384]{3,2,0,1:T(8,128)(2,1)S(1)}, u32[]{:S(2)}, u32[]{:S(2)}) collective-permute-start(bf16[4,2,16,384]{3,2,0,1:T(8,128)(2,1)S(1)} %get-tuple-element.26), channel_id=1, source_target_pairs={{0,8},{1,9},{2,10},{3,11},{4,12},{5,13},{6,14},{7,15},{8,16},{9,17... | collective-permute-start | bytes 294920 | tf_op jit(solution)/shard_map/ppermute | solution.py:245
  159.3 6.9 %collective-permute-start.4 = (bf16[4,2,16,384]{3,2,0,1:T(8,128)(2,1)S(1)}, bf16[4,2,16,384]{3,2,0,1:T(8,128)(2,1)S(1)}, u32[]{:S(2)}, u32[]{:S(2)}) collective-permute-start(bf16[4,2,16,384]{3,2,0,1:T(8,128)(2,1)S(1)} %get-tuple-element.25), channel_id=1, source_target_pairs={{0,16},{1,17},{2,18},{3,19},{4,20},{5,21},{6,22},{7,23},{8,24},{9,... | collective-permute-start | bytes 294920 | tf_op jit(solution)/shard_map/ppermute | solution.py:245
  161.1 5.9 %collective-permute-start.5 = (bf16[4,2,16,384]{3,2,0,1:T(8,128)(2,1)S(1)}, bf16[4,2,16,384]{3,2,0,1:T(8,128)(2,1)S(1)}, u32[]{:S(2)}, u32[]{:S(2)}) collective-permute-start(bf16[4,2,16,384]{3,2,0,1:T(8,128)(2,1)S(1)} %get-tuple-element.24), channel_id=1, source_target_pairs={{0,24},{1,25},{2,26},{3,27},{4,28},{5,29},{6,30},{7,31},{8,0},{9,1... | collective-permute-start | bytes 294920 | tf_op jit(solution)/shard_map/ppermute | solution.py:245
  167.8 1.4 collective-permute-start.6
  169.3 0.7 copy-start.7
  172.6 8.5 %collective-permute-start.7 = (f32[4,16,384]{2,1,0:T(8,128)}, f32[4,16,384]{2,1,0:T(8,128)S(1)}, u32[]{:S(2)}, u32[]{:S(2)}) collective-permute-start(f32[4,16,384]{2,1,0:T(8,128)} %get-tuple-element.18), channel_id=1, source_target_pairs={{0,32},{32,64},{64,96},{96,0},{1,33},{33,65},{65,97},{97,1},{2,34}... | collective-permute-start | bytes 294920 | tf_op jit(solution)/shard_map/ppermute | solution.py:259
  172.6 8.5 %collective-permute-start.8 = (f32[4,16,384]{2,1,0:T(8,128)}, f32[4,16,384]{2,1,0:T(8,128)S(1)}, u32[]{:S(2)}, u32[]{:S(2)}) collective-permute-start(f32[4,16,384]{2,1,0:T(8,128)} %get-tuple-element.19), channel_id=1, source_target_pairs={{0,64},{32,96},{64,0},{96,32},{1,65},{33,97},{65,1},{97,33},{2,66}... | collective-permute-start | bytes 294920 | tf_op jit(solution)/shard_map/ppermute | solution.py:259
  174.8 6.8 %collective-permute-start.9 = (f32[4,16,384]{2,1,0:T(8,128)}, f32[4,16,384]{2,1,0:T(8,128)S(1)}, u32[]{:S(2)}, u32[]{:S(2)}) collective-permute-start(f32[4,16,384]{2,1,0:T(8,128)} %get-tuple-element.20), channel_id=1, source_target_pairs={{0,96},{32,0},{64,32},{96,64},{1,97},{33,1},{65,33},{97,65},{2,98}... | collective-permute-start | bytes 294920 | tf_op jit(solution)/shard_map/ppermute | solution.py:259
where the time goes:
time: 184 us
  Pallas kernels  70.4 us (38%)
  waiting for transfers between devices  65.9 us (36%)
  starting transfers between devices  22.3 us (12%)
  other arithmetic  13.1 us (7%)
  local copies, waits for them, and re-layouts  11.2 us (6%)
    pallas_call x1, Pallas kernels, attention(): pl.pallas_call(attention_kernel, out_shape=(jax.ShapeDtypeStruct(q.shape,...  67.8 us
    all_to_all x1, waiting for transfers between devices, body(): lax.all_to_all(send, ('group', 'bank'), split_axis=0, concat_axis=0, tile...  51.9 us
    all_to_all x1, starting transfers between devices, body(): lax.all_to_all(send, ('group', 'bank'), split_axis=0, concat_axis=0, tile...  11.7 us
    select_n x1, other arithmetic, body(): send = share[tenant_bank_slot[tenant]]  10.7 us
    ppermute x3, waiting for transfers between devices, body(): part = lax.ppermute(sums[k], 'group', [(i, (i + k) % 4) for i in range(4)])  5.21 us
    ppermute x3, waiting for transfers between devices, body(): lax.ppermute(terms[k], 'bank', to_x(k))  4.8 us
    gather x2, local copies, waits for them, and re-layouts, body(): send = share[tenant_bank_slot[tenant]]  4.79 us
    ppermute x3, starting transfers between devices, body(): part = lax.ppermute(sums[k], 'group', [(i, (i + k) % 4) for i in range(4)])  3.89 us
  transfers between devices with their start and end apart: 11, of which 8 were waited for; matrix products, arithmetic and copies ran while one was open for 1% of the time, Pallas kernels for 0%

commit v1 on v0

v1 whole, which is shorter than its diff:
```python
import functools
import math

import jax
import jax.numpy as jnp
from jax import lax
from jax.experimental import pallas as pl
from jax.experimental.pallas import tpu as pltpu
from jax.sharding import PartitionSpec as P

SEQ = 256
PREFIX = 2048
HEAD = 128
KV_HEADS = 4
GROUP = 8
RANK = 16
KEY_BLOCK = 256
BLOCKS = PREFIX // KEY_BLOCK
ALL_KEYS = PREFIX + SEQ
LEAST_LIVE = 512
SLOTS = 16
MASKED = -1e30
SCALE = HEAD**-0.5
SCALE2 = SCALE * math.log2(math.e)
ADAPTER_SCALE = 2.0
ROWS_AT_ONCE = 16
UP = 128
DOWN = 160
TERM = 384
BANKS = 32
PART = 2


def lookup(table, position):
    matches = position[..., None] == jnp.arange(table.shape[0], dtype=jnp.int32)
    return jnp.sum(jnp.where(matches, table, 0), -1)


def dot(a, b, a_dim, b_dim):
    return lax.dot_general(
        a, b, (((a_dim,), (b_dim,)), ((), ())), preferred_element_type=jnp.float32
    )


def interleave(a, b):
    mixed, i, j = [], 0, 0
    while i < len(a) or j < len(b):
        if j == len(b) or (i < len(a) and i * len(b) <= j * len(a)):
            mixed.append(a[i])
            i += 1
        else:
            mixed.append(b[j])
            j += 1
    return mixed


def run(steps):
    for step in steps:
        step()


def attention_kernel(
    last,
    own, tenant, lengths, adapter_slot,
    q_ref, grad_ref, key_ref, value_ref, own_key_ref, own_value_ref, adapter_ref, mid_in_ref,
    *refs,
):
    if last:
        _, mid_so_far, up_so_far, x_ref, dq_ref, term_ref, *scratch = refs
    else:
        dq_ref, mid_ref, up_ref, *scratch = refs
    scores0, scores1, probs0, probs1, grads0, grads1, bias, partial, mid_sum, down = scratch
    g = pl.program_id(0)
    scores, probs, grads = (scores0, scores1), (probs0, probs1), (grads0, grads1)
    length = lengths[tenant[own[0]]]
    position = lax.broadcasted_iota(jnp.int32, bias.shape, 1)
    bias[...] = jnp.where(position < length, 0.0, MASKED)
    tiles = [(j, j + KEY_BLOCK) for j in range(0, ALL_KEYS, KEY_BLOCK)]

    def block(prefix_ref, own_ref, a, b):
        return prefix_ref[a:b, :] if a < PREFIX else own_ref[...]

    def pair(ref, p):
        return jnp.concatenate(
            [ref[:, i * HEAD : (i + 1) * HEAD] for i in (2 * p, 2 * p + 1)], axis=0
        )

    def front(p, s):
        q, grad = pair(q_ref, p), pair(grad_ref, p)

        def score(a, b):
            scores[s][:, a:b] = dot(q, block(key_ref, own_key_ref, a, b), 1, 1)

        def prob(a, b):
            probs[s][:, a:b] = dot(grad, block(value_ref, own_value_ref, a, b), 1, 1)

        return [functools.partial(f, a, b) for f in (score, prob) for a, b in tiles]

    def soft(s):
        def rows_at(r):
            rows = slice(r, r + ROWS_AT_ONCE)
            x = scores[s][rows, :]
            row = lax.broadcasted_iota(jnp.int32, (ROWS_AT_ONCE, SEQ), 0) + r % SEQ
            column = lax.broadcasted_iota(jnp.int32, (ROWS_AT_ONCE, SEQ), 1)
            x = jnp.concatenate(
                [
                    x[:, :LEAST_LIVE],
                    x[:, LEAST_LIVE:PREFIX] + bias[0:1, LEAST_LIVE:],
                    jnp.where(column <= row, x[:, PREFIX:], MASKED),
                ],
                axis=1,
            )
            top = jnp.max(x, axis=-1, keepdims=True)
            e = jnp.exp2(x * SCALE2 - top * SCALE2)
            inverse = 1.0 / jnp.sum(e, axis=-1, keepdims=True)
            prob_grad = probs[s][rows, :]
            delta = jnp.sum(e * prob_grad, axis=-1, keepdims=True) * inverse
            grads[s][rows, :] = ((e * inverse) * (prob_grad - delta)).astype(jnp.bfloat16)

        return [functools.partial(rows_at, r) for r in range(0, 2 * SEQ, ROWS_AT_ONCE)]

    def back(p, s):
        def part(i, a, b):
            x = dot(grads[s][:, a:b], block(key_ref, own_key_ref, a, b), 1, 0)
            if i:
                x += partial[...]
            if b < ALL_KEYS:
                partial[...] = x
            else:
                x = (x * SCALE).astype(jnp.bfloat16)
                for k in range(2):
                    dq_ref[:, (2 * p + k) * HEAD : (2 * p + k + 1) * HEAD] = x[k * SEQ : (k + 1) * SEQ]

        return [functools.partial(part, i, a, b) for i, (a, b) in enumerate(tiles)]

    run(front(0, 0))
    run(interleave(front(1, 1), soft(0)))
    run(interleave(front(2, 0) + back(0, 0), soft(1)))
    run(interleave(front(3, 1) + back(1, 1), soft(0)))
    run(interleave(back(2, 0), soft(1)))
    run(back(3, 1))

    @pl.when(g == 0)
    def _():
        mid_sum[...] = mid_so_far[...] if last else jnp.zeros_like(mid_sum)

    dq = dq_ref[...]
    mid_sum[...] += dot(dq, adapter_ref[0], 1, 1)
    up = (ADAPTER_SCALE * dot(mid_in_ref[...], dq, 0, 0)).astype(jnp.bfloat16)
    for i in range(GROUP):
        piece = up[:, i * UP : (i + 1) * UP]
        if last:
            term_ref[BANKS // 2 + g * GROUP + i, :, 0:UP] = piece
        else:
            up_ref[i] = piece

    @pl.when(g == PART - 1)
    def _():
        if last:
            mid = mid_sum[...].astype(jnp.bfloat16)
            down[...] = ADAPTER_SCALE * dot(mid, x_ref[...], 0, 0)
            for b in range(BANKS):
                if b < BANKS // 2:
                    term_ref[b, :, 0:UP] = up_so_far[b]
                term_ref[b, :, UP : UP + DOWN] = down[:, b * DOWN : (b + 1) * DOWN].astype(jnp.bfloat16)
                term_ref[b, :, UP + DOWN :] = jnp.zeros((RANK, TERM - UP - DOWN), jnp.bfloat16)
        else:
            mid_ref[...] = mid_sum[...]


def attention(first, own, tenant, lengths, adapter_slot, q, grad, pairs, own_key, own_value, adapters, mid_in, earlier):
    last = bool(earlier)

    def wide(shape):
        return pl.BlockSpec(shape, lambda g, *_: (0, first + g))

    def whole(shape):
        return pl.BlockSpec(shape, lambda g, *_: (0,) * len(shape))

    def adapter_at(g, own, tenant, lengths, adapter_slot):
        return (adapter_slot[tenant[own[0]]], 0, first + g)

    dq = jax.ShapeDtypeStruct(q.shape, jnp.bfloat16)
    if last:
        out_shape = (dq, jax.ShapeDtypeStruct((BANKS, RANK, TERM), jnp.bfloat16))
        out_specs = (wide((SEQ, GROUP * HEAD)), whole((BANKS, RANK, TERM)))
        more = [pl.BlockSpec(memory_space=pl.ANY)] + [whole(e.shape) for e in earlier[1:]]
    else:
        out_shape = (
            dq,
            jax.ShapeDtypeStruct((SEQ, RANK), jnp.float32),
            jax.ShapeDtypeStruct((BANKS // 2, RANK, UP), jnp.bfloat16),
        )
        out_specs = (
            wide((SEQ, GROUP * HEAD)),
            whole((SEQ, RANK)),
            pl.BlockSpec((GROUP, RANK, UP), lambda g, *_: (g, 0, 0)),
        )
        more = []
    return pl.pallas_call(
        functools.partial(attention_kernel, last),
        out_shape=out_shape,
        grid_spec=pltpu.PrefetchScalarGridSpec(
            num_scalar_prefetch=4,
            grid=(PART,),
            in_specs=[
                wide((SEQ, GROUP * HEAD)),
                wide((SEQ, GROUP * HEAD)),
                pl.BlockSpec((PREFIX, HEAD), lambda g, *_: (0, g)),
                pl.BlockSpec((PREFIX, HEAD), lambda g, *_: (0, PART + g)),
                wide((SEQ, HEAD)),
                wide((SEQ, HEAD)),
                pl.BlockSpec((1, RANK, GROUP * HEAD), adapter_at),
                whole(mid_in.shape),
                *more,
            ],
            out_specs=out_specs,
            scratch_shapes=[
                *[pltpu.VMEM((2 * SEQ, ALL_KEYS), jnp.float32)] * 4,
                *[pltpu.VMEM((2 * SEQ, ALL_KEYS), jnp.bfloat16)] * 2,
                pltpu.VMEM((8, PREFIX), jnp.float32),
                pltpu.VMEM((2 * SEQ, HEAD), jnp.float32),
                pltpu.VMEM((SEQ, RANK), jnp.float32),
                pltpu.VMEM((RANK, BANKS * DOWN), jnp.float32),
            ],
        ),
        input_output_aliases={12: 0} if last else {},
        compiler_params=pltpu.CompilerParams(vmem_limit_bytes=56 << 20),
        cost_estimate=pl.CostEstimate(flops=15_000_000_000, bytes_accessed=8_000_000, transcendentals=10_000_000),
        name="attention_last" if last else "attention_first",
    )(own, tenant, lengths, adapter_slot, q, grad, pairs, pairs, own_key, own_value, adapters, mid_in, *earlier)


def sum_kernel(own, tenant, adapter_slot, terms_ref, a0_ref, a1_ref, a2_ref, a3_ref, total):
    total[...] = jnp.zeros_like(total)
    mine = own[0] // BANKS
    for i in range(BANKS):
        slot = adapter_slot[tenant[mine * BANKS + i]]
        total[slot] += terms_ref[i].astype(jnp.float32)
    for k, ref in enumerate((a0_ref, a1_ref, a2_ref, a3_ref)):
        start = lax.rem(mine + k, 4) * 4
        for i in range(4):
            ref[i] = total[start + i].astype(ref.dtype)


def sum_terms(own, tenant, adapter_slot, terms):
    shape = (4, RANK, TERM)
    return pl.pallas_call(
        sum_kernel,
        out_shape=[
            jax.ShapeDtypeStruct(shape, jnp.bfloat16 if k else jnp.float32) for k in range(4)
        ],
        grid_spec=pltpu.PrefetchScalarGridSpec(
            num_scalar_prefetch=3,
            grid=(1,),
            in_specs=[pl.BlockSpec(terms.shape, lambda i, *_: (0, 0, 0))],
            out_specs=[pl.BlockSpec(shape, lambda i, *_: (0, 0, 0))] * 4,
            scratch_shapes=[pltpu.VMEM((SLOTS, RANK, TERM), jnp.float32)],
        ),
        name="sum_terms",
    )(own, tenant, adapter_slot, terms)


def body(
    normed_layer_input,
    input_times_down,
    queries,
    row_own_keys,
    row_own_values,
    output_gradient,
    prefix_key_bank,
    prefix_value_bank,
    live_prefix_length,
    tenant,
    tenant_bank_slot,
    tenant_adapter_slot,
    query_up_adapters,
):
    own = lax.axis_index(("group", "bank")).astype(jnp.int32)[None]
    bank_slot = lookup(tenant_bank_slot, tenant)
    width = PART * HEAD
    pairs = []
    for first in range(0, KV_HEADS, PART):
        columns = slice(first * HEAD, first * HEAD + width)
        share = jnp.concatenate([prefix_key_bank[:, :, columns], prefix_value_bank[:, :, columns]], -1)
        got = lax.all_to_all(share[bank_slot], ("group", "bank"), split_axis=0, concat_axis=0, tiled=True)
        pairs.append(got.reshape(PREFIX, 2 * width))
    call = functools.partial(
        attention, own=own, tenant=tenant, lengths=live_prefix_length, adapter_slot=tenant_adapter_slot,
        q=queries[0], grad=output_gradient[0], own_key=row_own_keys[0], own_value=row_own_values[0],
        adapters=query_up_adapters, mid_in=input_times_down[0],
    )
    dq, mid, up = call(first=0, pairs=pairs[0], earlier=())
    dq, terms = call(first=PART, pairs=pairs[1], earlier=(dq, mid, up, normed_layer_input[0]))
    terms = lax.all_to_all(terms, "bank", split_axis=0, concat_axis=0, tiled=True)
    sums = sum_terms(own, tenant, tenant_adapter_slot, terms)
    parts = [sums[0]] + [
        lax.ppermute(sums[k], "group", [(i, (i + k) % 4) for i in range(4)]) for k in range(1, 4)
    ]

    def total(columns):
        return sum(p[:, :, columns].astype(jnp.float32) for p in parts)

    return dq[None], total(slice(UP, UP + DOWN)), total(slice(0, UP))


def solution(mesh):
    rows = P(("group", "bank"), None, None)
    return jax.shard_map(
        body,
        mesh=mesh,
        in_specs=(rows,) * 6 + (P(None, ("group", "bank"), None),) * 2 + (P(),) * 5,
        out_specs=(rows, P("group", None, "bank"), P("group", None, "bank")),
        check_vma=False,
    )
```

time: 184 us -> 141 us (0.77)
  waiting for transfers between devices: 65.9 us -> 33.1 us
  blocking collectives: 0 us -> 15.5 us
  Pallas kernels: 70.4 us -> 59 us
  other arithmetic: 13.1 us -> 3.68 us
  local copies, waits for them, and re-layouts: 11.2 us -> 5.88 us
    all_to_all x1 -> x2, waiting for transfers between devices: 51.9 us -> 30.2 us  [body(): lax.all_to_all(share[bank_slot], ('group', 'bank'), split_axis=0, concat_...]
    all_to_all x0 -> x1, blocking collectives: none -> 15.5 us  [body(): lax.all_to_all(terms, 'bank', split_axis=0, concat_axis=0, tiled=True)]
    pallas_call x2 -> x3, Pallas kernels: 70.4 us -> 59 us  [the longest x2 56.4 us: attention(): pl.pallas_call(functools.partial(attention_kernel, last), out_shape=out_s...]
    ppermute x10 -> x3, waiting for transfers between devices: 14.1 us -> 2.91 us  [body(): lax.ppermute(sums[k], 'group', [(i, (i + k) % 4) for i in range(4)])]
    select_n x3 -> x1, other arithmetic: 10.8 us -> 0.01 us  [body(): share[bank_slot]]
    all_to_all x1 -> x2, starting transfers between devices: 11.7 us -> 17 us  [body(): lax.all_to_all(share[bank_slot], ('group', 'bank'), split_axis=0, concat_...]
    ppermute x10 -> x3, starting transfers between devices: 10.6 us -> 5.73 us  [body(): lax.ppermute(sums[k], 'group', [(i, (i + k) % 4) for i in range(4)])]
    gather x4 -> x2, local copies, waits for them, and re-layouts: 6.69 us -> 4.01 us  [body(): share[bank_slot]]
  transfers between devices with their start and end apart: 11 -> 5, of which waited for: 8 -> 4; matrix products, arithmetic and copies ran while one was open for 1% -> 2% of each run, Pallas kernels for 0% -> 19%
where the time goes in v1:
time: 141 us; the launch traced here: 140 us
  Pallas kernels  59 us (42%)
  waiting for transfers between devices  33.1 us (23%)
  starting transfers between devices  22.7 us (16%)
  blocking collectives  15.5 us (11%)
  local copies, waits for them, and re-layouts  5.88 us (4%)
  other arithmetic  3.68 us (3%)
    pallas_call x2, Pallas kernels, attention(): pl.pallas_call(functools.partial(attention_kernel, last), out_shape=out_s...  56.4 us
    all_to_all x2, waiting for transfers between devices, body(): lax.all_to_all(share[bank_slot], ('group', 'bank'), split_axis=0, concat_...  30.2 us
    all_to_all x2, starting transfers between devices, body(): lax.all_to_all(share[bank_slot], ('group', 'bank'), split_axis=0, concat_...  17 us
    all_to_all x1, blocking collectives, body(): lax.all_to_all(terms, 'bank', split_axis=0, concat_axis=0, tiled=True)  15.5 us
    ppermute x3, starting transfers between devices, body(): lax.ppermute(sums[k], 'group', [(i, (i + k) % 4) for i in range(4)])  5.73 us
    gather x2, local copies, waits for them, and re-layouts, body(): share[bank_slot]  4.01 us
    ppermute x3, waiting for transfers between devices, body(): lax.ppermute(sums[k], 'group', [(i, (i + k) % 4) for i in range(4)])  2.91 us
    add x2, other arithmetic, total(): return sum((p[:, :, columns].astype(jnp.float32) for p in parts))  2.87 us
  transfers between devices with their start and end apart: 5, of which 4 were waited for; matrix products, arithmetic and copies ran while one was open for 2% of the time, Pallas kernels for 19%

profile of v1, /device:TPU:0, one launch (start us, length us, event | category | flops | bytes accessed | tf_op | source)
XLA Modules:
  0.0 140.5 jit_solution(18279424282172771492)
XLA Ops:
  0.6 0.8 select_reduce_fusion
  1.4 1.1 fusion.1
  2.6 2.0 %gather_fusion.1 = bf16[128,16,512]{2,1,0:T(8,128)(2,1)} fusion(bf16[16,16,512]{2,1,0:T(8,128)(2,1)S(1)} %pad_maximum_fusion.1, s32[1024]{0:T(1024)S(1)} %pad_clamp_fusion), kind=kCustom, calls=%fused_computation.1 | custom fusion | bytes 4194816 | tf_op jit(solution)/shard_map/gather | solution.py:286
  4.6 11.1 %all-to-all-start.1 = ((bf16[128,16,512]{2,1,0:T(8,128)(2,1)}), bf16[128,16,512]{2,1,0:T(8,128)(2,1)S(1)}, u32[]{:S(2)}, u32[]{:S(2)}) async-start(bf16[128,16,512]{2,1,0:T(8,128)(2,1)} %gather_fusion.1), calls=%async_computation.1 | async-start | bytes 4194304 | tf_op jit(solution)/shard_map/all_to_all | solution.py:286
  15.7 2.0 %gather_fusion = bf16[128,16,512]{2,1,0:T(8,128)(2,1)} fusion(bf16[16,16,512]{2,1,0:T(8,128)(2,1)S(1)} %pad_maximum_fusion, s32[1024]{0:T(1024)S(1)} %pad_clamp_fusion), kind=kCustom, calls=%fused_computation | custom fusion | bytes 4194816 | tf_op jit(solution)/shard_map/gather | solution.py:286
  17.7 0.0 copy-start.1
  17.8 28.4 %all-to-all-done.1 = bf16[128,16,512]{2,1,0:T(8,128)(2,1)S(1)} async-done(((bf16[128,16,512]{2,1,0:T(8,128)(2,1)}), bf16[128,16,512]{2,1,0:T(8,128)(2,1)S(1)}, u32[]{:S(2)}, u32[]{:S(2)}) %all-to-all-start.1) | async-done | bytes 2097184 | tf_op jit(solution)/shard_map/all_to_all | solution.py:286
  46.1 5.8 %all-to-all-start = ((bf16[128,16,512]{2,1,0:T(8,128)(2,1)}), bf16[128,16,512]{2,1,0:T(8,128)(2,1)}, u32[]{:S(2)}, u32[]{:S(2)}) async-start(bf16[128,16,512]{2,1,0:T(8,128)(2,1)} %gather_fusion), calls=%async_computation | async-start | bytes 4194304 | tf_op jit(solution)/shard_map/all_to_all | solution.py:286
  51.9 0.0 copy-done
  52.0 0.0 copy-done.1
  52.0 0.7 copy.18
  52.7 27.3 %attention_first.1 = (bf16[256,4096]{1,0:T(8,128)(2,1)}, f32[256,16]{1,0:T(8,128)}, bf16[16,16,128]{2,1,0:T(8,128)(2,1)}) custom-call(s32[1]{0:T(128)} %bitcast.own, s32[128]{0:T(128)} %tenant.5, s32[16]{0:T(128)} %lengths.3, s32[16]{0:T(128)} %adapter_slot.5, bf16[256,4096]{1,0:T(8,128)(2,1)} %bitcast.19, bf16[256,4096]{1,0:T(8,128)(2,1)} %bitcast.21, ...), custom_call_target="tpu_custom_call" | custom-call | flops 15000000512 | bytes 8000000 | tf_op jit(solution)/shard_map/attention_first/pallas_call | solution.py:200
  80.1 1.8 %all-to-all-done = bf16[128,16,512]{2,1,0:T(8,128)(2,1)} async-done(((bf16[128,16,512]{2,1,0:T(8,128)(2,1)}), bf16[128,16,512]{2,1,0:T(8,128)(2,1)}, u32[]{:S(2)}, u32[]{:S(2)}) %all-to-all-start) | async-done | bytes 2097184 | tf_op jit(solution)/shard_map/all_to_all | solution.py:286
  81.9 29.0 %attention_last.1 = (bf16[256,4096]{1,0:T(8,128)(2,1)}, bf16[32,16,384]{2,1,0:T(8,128)(2,1)}) custom-call(s32[1]{0:T(128)} %bitcast.own, s32[128]{0:T(128)} %tenant.5, s32[16]{0:T(128)} %lengths.3, s32[16]{0:T(128)} %adapter_slot.5, bf16[256,4096]{1,0:T(8,128)(2,1)} %bitcast.20, bf16[256,4096]{1,0:T(8,128)(2,1)} %bitcast.22, ...), custom_call_target="tpu_custom_call", output_to_operand_aliasing={{0}: (12, {})} | custom-call | flops 15000000512 | bytes 8000000 | tf_op jit(solution)/shard_map/attention_last/pallas_call | solution.py:200
  110.9 15.5 %all_to_all.15.terms_ref = bf16[32,16,384]{2,1,0:T(8,128)(2,1)} all-to-all(bf16[32,16,384]{2,1,0:T(8,128)(2,1)} %get-tuple-element.16), channel_id=1, replica_groups=mesh['group'=4,'bank'=32] {'bank'}, dimensions={0} | all-to-all | bytes 786432 | tf_op jit(solution)/shard_map/all_to_all | solution.py:295
  126.4 2.6 %sum_terms.1 = (f32[4,16,384]{2,1,0:T(8,128)}, bf16[4,16,384]{2,1,0:T(8,128)(2,1)}, bf16[4,16,384]{2,1,0:T(8,128)(2,1)}, bf16[4,16,384]{2,1,0:T(8,128)(2,1)}) custom-call(s32[1]{0:T(128)} %bitcast.own, s32[128]{0:T(128)} %tenant.5, s32[16]{0:T(128)} %adapter_slot.5, bf16[32,16,384]{2,1,0:T(8,128)(2,1)} %all_to_all.15.terms_ref), custom_call_target="tpu_custom_call" | custom-call | tf_op jit(solution)/shard_map/sum_terms/pallas_call | solution.py:248
  129.0 1.5 %collective-permute-start = (bf16[4,16,384]{2,1,0:T(8,128)(2,1)}, bf16[4,16,384]{2,1,0:T(8,128)(2,1)S(1)}, u32[]{:S(2)}, u32[]{:S(2)}) collective-permute-start(bf16[4,16,384]{2,1,0:T(8,128)(2,1)} %get-tuple-element.18), channel_id=1, source_target_pairs={{0,32},{32,64},{64,96},{96,0},{1,33},{33,65},{65,97},{97,1},{2,34}... | collective-permute-start | bytes 147464 | tf_op jit(solution)/shard_map/ppermute | solution.py:298
  130.5 2.8 %collective-permute-start.1 = (bf16[4,16,384]{2,1,0:T(8,128)(2,1)}, bf16[4,16,384]{2,1,0:T(8,128)(2,1)S(1)}, u32[]{:S(2)}, u32[]{:S(2)}) collective-permute-start(bf16[4,16,384]{2,1,0:T(8,128)(2,1)} %get-tuple-element.19), channel_id=1, source_target_pairs={{0,64},{32,96},{64,0},{96,32},{1,65},{33,97},{65,1},{97,33},{2,66}... | collective-permute-start | bytes 147464 | tf_op jit(solution)/shard_map/ppermute | solution.py:298
  133.3 1.4 collective-permute-start.2
  134.7 0.0 collective-permute-done
  134.7 1.6 %collective-permute-done.1 = bf16[4,16,384]{2,1,0:T(8,128)(2,1)S(1)} collective-permute-done((bf16[4,16,384]{2,1,0:T(8,128)(2,1)}, bf16[4,16,384]{2,1,0:T(8,128)(2,1)S(1)}, u32[]{:S(2)}, u32[]{:S(2)}) %collective-permute-start.1) | collective-permute-done | bytes 49184 | tf_op jit(solution)/shard_map/ppermute | solution.py:298
  136.4 1.3 collective-permute-done.2
  137.6 1.4 convert_add_fusion.1
  139.0 1.5 %convert_add_fusion = f32[4,16,160]{2,1,0:T(8,128)} fusion(f32[4,16,384]{2,1,0:T(8,128)} %get-tuple-element.17, bf16[4,16,384]{2,1,0:T(8,128)(2,1)S(1)} %collective-permute-done.2, bf16[4,16,384]{2,1,0:T(8,128)(2,1)S(1)} %collective-permute-done.1, bf16[4,16,384]{2,1,0:T(8,128)(2,1)S(1)} %collective-permute-done), kind=kLoop, calls=%fused_computation.4 | loop fusion | flops 61440 | bytes 143360 | tf_op jit(solution)/shard_map/add | solution.py:302
  (5 shorter events, 0.1 us)
Async XLA Ops:
  4.6 41.5 %all-to-all-start.1 = ((bf16[128,16,512]{2,1,0:T(8,128)(2,1)}), bf16[128,16,512]{2,1,0:T(8,128)(2,1)S(1)}, u32[]{:S(2)}, u32[]{:S(2)}) async-start(bf16[128,16,512]{2,1,0:T(8,128)(2,1)} %gather_fusion.1), calls=%async_computation.1 | async-start | bytes 4194304 | tf_op jit(solution)/shard_map/all_to_all | solution.py:286
  17.7 34.2 %copy-start.1 = (bf16[1,256,16]{1,2,0:T(8,128)(2,1)S(1)}, bf16[1,256,16]{1,2,0:T(8,128)(2,1)}, u32[]{:S(2)}) copy-start(bf16[1,256,16]{1,2,0:T(8,128)(2,1)} %param.14) | copy-start | bytes 24580
  46.1 5.8 %copy-start = (bf16[128,16,512]{2,1,0:T(8,128)(2,1)}, bf16[128,16,512]{2,1,0:T(8,128)(2,1)S(1)}, u32[]{:S(2)}) copy-start(bf16[128,16,512]{2,1,0:T(8,128)(2,1)S(1)} %all-to-all-done.1) | copy-start | bytes 6291460
  46.1 35.8 %all-to-all-start = ((bf16[128,16,512]{2,1,0:T(8,128)(2,1)}), bf16[128,16,512]{2,1,0:T(8,128)(2,1)}, u32[]{:S(2)}, u32[]{:S(2)}) async-start(bf16[128,16,512]{2,1,0:T(8,128)(2,1)} %gather_fusion), calls=%async_computation | async-start | bytes 4194304 | tf_op jit(solution)/shard_map/all_to_all | solution.py:286
  129.0 5.7 %collective-permute-start = (bf16[4,16,384]{2,1,0:T(8,128)(2,1)}, bf16[4,16,384]{2,1,0:T(8,128)(2,1)S(1)}, u32[]{:S(2)}, u32[]{:S(2)}) collective-permute-start(bf16[4,16,384]{2,1,0:T(8,128)(2,1)} %get-tuple-element.18), channel_id=1, source_target_pairs={{0,32},{32,64},{64,96},{96,0},{1,33},{33,65},{65,97},{97,1},{2,34}... | collective-permute-start | bytes 147464 | tf_op jit(solution)/shard_map/ppermute | solution.py:298
  130.5 5.8 %collective-permute-start.1 = (bf16[4,16,384]{2,1,0:T(8,128)(2,1)}, bf16[4,16,384]{2,1,0:T(8,128)(2,1)S(1)}, u32[]{:S(2)}, u32[]{:S(2)}) collective-permute-start(bf16[4,16,384]{2,1,0:T(8,128)(2,1)} %get-tuple-element.19), channel_id=1, source_target_pairs={{0,64},{32,96},{64,0},{96,32},{1,65},{33,97},{65,1},{97,33},{2,66}... | collective-permute-start | bytes 147464 | tf_op jit(solution)/shard_map/ppermute | solution.py:298
  133.3 4.3 %collective-permute-start.2 = (bf16[4,16,384]{2,1,0:T(8,128)(2,1)}, bf16[4,16,384]{2,1,0:T(8,128)(2,1)S(1)}, u32[]{:S(2)}, u32[]{:S(2)}) collective-permute-start(bf16[4,16,384]{2,1,0:T(8,128)(2,1)} %get-tuple-element.20), channel_id=1, source_target_pairs={{0,96},{32,0},{64,32},{96,64},{1,97},{33,1},{65,33},{97,65},{2,98}... | collective-permute-start | bytes 147464 | tf_op jit(solution)/shard_map/ppermute | solution.py:298

commit v2 on v1

--- a/solution.py
+++ b/solution.py
@@ -135,10 +135,13 @@
 
     run(front(0, 0))
     run(interleave(front(1, 1), soft(0)))
-    run(interleave(front(2, 0) + back(0, 0), soft(1)))
-    run(interleave(front(3, 1) + back(1, 1), soft(0)))
+    run(interleave(back(0, 0) + front(2, 0), soft(1)))
+    run(interleave(back(1, 1) + front(3, 1), soft(0)))
     run(interleave(back(2, 0), soft(1)))
-    run(back(3, 1))
+    x = dot(grads1[:, :PREFIX], key_ref[...], 1, 0) + dot(grads1[:, PREFIX:], own_key_ref[...], 1, 0)
+    x = (x * SCALE).astype(jnp.bfloat16)
+    for k in range(2):
+        dq_ref[:, (6 + k) * HEAD : (7 + k) * HEAD] = x[k * SEQ : (k + 1) * SEQ]
 
     @pl.when(g == 0)
     def _():
@@ -261,6 +264,23 @@
     )(own, tenant, adapter_slot, terms)
 
 
+def add_kernel(a0_ref, a1_ref, a2_ref, a3_ref, down_ref, up_ref):
+    total = a0_ref[...]
+    for ref in (a1_ref, a2_ref, a3_ref):
+        total += ref[...].astype(jnp.float32)
+    up_ref[...] = total[:, :, :UP]
+    down_ref[...] = total[:, :, UP : UP + DOWN]
+
+
+def add_groups(parts):
+    shape = parts[0].shape[:2]
+    return pl.pallas_call(
+        add_kernel,
+        out_shape=[jax.ShapeDtypeStruct((*shape, width), jnp.float32) for width in (DOWN, UP)],
+        name="add_groups",
+    )(*parts)
+
+
 def body(
     normed_layer_input,
     input_times_down,
@@ -298,10 +318,8 @@
         lax.ppermute(sums[k], "group", [(i, (i + k) % 4) for i in range(4)]) for k in range(1, 4)
     ]
 
-    def total(columns):
-        return sum(p[:, :, columns].astype(jnp.float32) for p in parts)
-
-    return dq[None], total(slice(UP, UP + DOWN)), total(slice(0, UP))
+    down_grad, up_grad = add_groups(parts)
+    return dq[None], down_grad, up_grad
 
 
 def solution(mesh):

time: 141 us -> 138 us (0.979)
  other arithmetic: 3.68 us -> 0.81 us
    add x2 -> x0, other arithmetic: 2.87 us -> none  [total(): return sum((p[:, :, columns].astype(jnp.float32) for p in parts))]
    pallas_call x2, Pallas kernels: 56.4 us -> 54.2 us  [attention(): pl.pallas_call(functools.partial(attention_kernel, last), out_shape=out_s...]
    pallas_call x0 -> x1, Pallas kernels: none -> 1.58 us  [add_groups(): pl.pallas_call(add_kernel, out_shape=[jax.ShapeDtypeStruct((*shape, width...]
  transfers between devices with their start and end apart: 5 -> 5, of which waited for: 4 -> 5; matrix products, arithmetic and copies ran while one was open for 2% -> 2% of each run, Pallas kernels for 19% -> 19%
where the time goes in v2:
time: 138 us
  Pallas kernels  58.4 us (42%)
  waiting for transfers between devices  34.2 us (25%)
  starting transfers between devices  22.2 us (16%)
  blocking collectives  14.9 us (11%)
  local copies, waits for them, and re-layouts  6.49 us (5%)
    pallas_call x2, Pallas kernels, attention(): pl.pallas_call(functools.partial(attention_kernel, last), out_shape=out_s...  54.2 us
    all_to_all x2, waiting for transfers between devices, body(): lax.all_to_all(share[bank_slot], ('group', 'bank'), split_axis=0, concat_...  31.3 us
    all_to_all x2, starting transfers between devices, body(): lax.all_to_all(share[bank_slot], ('group', 'bank'), split_axis=0, concat_...  17 us
    all_to_all x1, blocking collectives, body(): lax.all_to_all(terms, 'bank', split_axis=0, concat_axis=0, tiled=True)  14.9 us
    ppermute x3, starting transfers between devices, body(): lax.ppermute(sums[k], 'group', [(i, (i + k) % 4) for i in range(4)])  5.22 us
    gather x2, local copies, waits for them, and re-layouts, body(): share[bank_slot]  4 us
    ppermute x3, waiting for transfers between devices, body(): lax.ppermute(sums[k], 'group', [(i, (i + k) % 4) for i in range(4)])  2.9 us
  transfers between devices with their start and end apart: 5, of which 5 were waited for; matrix products, arithmetic and copies ran while one was open for 2% of the time, Pallas kernels for 19%

profile of v2, /device:TPU:0, one launch (start us, length us, event | category | flops | bytes accessed | tf_op | source)
XLA Modules:
  0.0 137.6 jit_solution(4790860637562063690)
XLA Ops:
  0.6 0.8 select_reduce_fusion
  1.4 1.1 fusion.1
  2.6 2.0 %gather_fusion.1 = bf16[128,16,512]{2,1,0:T(8,128)(2,1)} fusion(bf16[16,16,512]{2,1,0:T(8,128)(2,1)S(1)} %pad_maximum_fusion.1, s32[1024]{0:T(1024)S(1)} %pad_clamp_fusion), kind=kCustom, calls=%fused_computation.1 | custom fusion | bytes 4194816 | tf_op jit(solution)/shard_map/gather | solution.py:306
  4.6 11.1 %all-to-all-start.1 = ((bf16[128,16,512]{2,1,0:T(8,128)(2,1)}), bf16[128,16,512]{2,1,0:T(8,128)(2,1)S(1)}, u32[]{:S(2)}, u32[]{:S(2)}) async-start(bf16[128,16,512]{2,1,0:T(8,128)(2,1)} %gather_fusion.1), calls=%async_computation.1 | async-start | bytes 4194304 | tf_op jit(solution)/shard_map/all_to_all | solution.py:306
  15.7 2.0 %gather_fusion = bf16[128,16,512]{2,1,0:T(8,128)(2,1)} fusion(bf16[16,16,512]{2,1,0:T(8,128)(2,1)S(1)} %pad_maximum_fusion, s32[1024]{0:T(1024)S(1)} %pad_clamp_fusion), kind=kCustom, calls=%fused_computation | custom fusion | bytes 4194816 | tf_op jit(solution)/shard_map/gather | solution.py:306
  17.7 28.4 %all-to-all-done.1 = bf16[128,16,512]{2,1,0:T(8,128)(2,1)S(1)} async-done(((bf16[128,16,512]{2,1,0:T(8,128)(2,1)}), bf16[128,16,512]{2,1,0:T(8,128)(2,1)S(1)}, u32[]{:S(2)}, u32[]{:S(2)}) %all-to-all-start.1) | async-done | bytes 2097184 | tf_op jit(solution)/shard_map/all_to_all | solution.py:306
  46.1 5.8 %all-to-all-start = ((bf16[128,16,512]{2,1,0:T(8,128)(2,1)}), bf16[128,16,512]{2,1,0:T(8,128)(2,1)}, u32[]{:S(2)}, u32[]{:S(2)}) async-start(bf16[128,16,512]{2,1,0:T(8,128)(2,1)} %gather_fusion), calls=%async_computation | async-start | bytes 4194304 | tf_op jit(solution)/shard_map/all_to_all | solution.py:306
  51.9 0.0 copy-done
  51.9 0.0 copy-done.4
  52.0 0.7 copy.18
  52.7 26.3 %attention_first.1 = (bf16[256,4096]{1,0:T(8,128)(2,1)}, f32[256,16]{1,0:T(8,128)}, bf16[16,16,128]{2,1,0:T(8,128)(2,1)}) custom-call(s32[1]{0:T(128)} %bitcast.own, s32[128]{0:T(128)} %tenant.5, s32[16]{0:T(128)} %lengths.3, s32[16]{0:T(128)} %adapter_slot.5, bf16[256,4096]{1,0:T(8,128)(2,1)} %bitcast.19, bf16[256,4096]{1,0:T(8,128)(2,1)} %bitcast.21, ...), custom_call_target="tpu_custom_call" | custom-call | flops 15000000512 | bytes 8000000 | tf_op jit(solution)/shard_map/attention_first/pallas_call | solution.py:203
  78.9 2.9 %all-to-all-done = bf16[128,16,512]{2,1,0:T(8,128)(2,1)} async-done(((bf16[128,16,512]{2,1,0:T(8,128)(2,1)}), bf16[128,16,512]{2,1,0:T(8,128)(2,1)}, u32[]{:S(2)}, u32[]{:S(2)}) %all-to-all-start) | async-done | bytes 2097184 | tf_op jit(solution)/shard_map/all_to_all | solution.py:306
  81.9 28.0 %attention_last.1 = (bf16[256,4096]{1,0:T(8,128)(2,1)}, bf16[32,16,384]{2,1,0:T(8,128)(2,1)}) custom-call(s32[1]{0:T(128)} %bitcast.own, s32[128]{0:T(128)} %tenant.5, s32[16]{0:T(128)} %lengths.3, s32[16]{0:T(128)} %adapter_slot.5, bf16[256,4096]{1,0:T(8,128)(2,1)} %bitcast.20, bf16[256,4096]{1,0:T(8,128)(2,1)} %bitcast.22, ...), custom_call_target="tpu_custom_call", output_to_operand_aliasing={{0}: (12, {})} | custom-call | flops 15000000512 | bytes 8000000 | tf_op jit(solution)/shard_map/attention_last/pallas_call | solution.py:203
  109.9 14.9 %all_to_all.15.terms_ref = bf16[32,16,384]{2,1,0:T(8,128)(2,1)} all-to-all(bf16[32,16,384]{2,1,0:T(8,128)(2,1)} %get-tuple-element.18), channel_id=1, replica_groups=mesh['group'=4,'bank'=32] {'bank'}, dimensions={0} | all-to-all | bytes 786432 | tf_op jit(solution)/shard_map/all_to_all | solution.py:315
  124.7 2.6 %sum_terms.1 = (f32[4,16,384]{2,1,0:T(8,128)}, bf16[4,16,384]{2,1,0:T(8,128)(2,1)}, bf16[4,16,384]{2,1,0:T(8,128)(2,1)}, bf16[4,16,384]{2,1,0:T(8,128)(2,1)}) custom-call(s32[1]{0:T(128)} %bitcast.own, s32[128]{0:T(128)} %tenant.5, s32[16]{0:T(128)} %adapter_slot.5, bf16[32,16,384]{2,1,0:T(8,128)(2,1)} %all_to_all.15.terms_ref), custom_call_target="tpu_custom_call" | custom-call | tf_op jit(solution)/shard_map/sum_terms/pallas_call | solution.py:251
  127.3 1.0 collective-permute-start
  128.3 2.8 %collective-permute-start.1 = (bf16[4,16,384]{2,1,0:T(8,128)(2,1)}, bf16[4,16,384]{2,1,0:T(8,128)(2,1)S(1)}, u32[]{:S(2)}, u32[]{:S(2)}) collective-permute-start(bf16[4,16,384]{2,1,0:T(8,128)(2,1)} %get-tuple-element.21), channel_id=1, source_target_pairs={{0,64},{32,96},{64,0},{96,32},{1,65},{33,97},{65,1},{97,33},{2,66}... | collective-permute-start | bytes 147464 | tf_op jit(solution)/shard_map/ppermute | solution.py:318
  131.1 1.4 %collective-permute-start.2 = (bf16[4,16,384]{2,1,0:T(8,128)(2,1)}, bf16[4,16,384]{2,1,0:T(8,128)(2,1)S(1)}, u32[]{:S(2)}, u32[]{:S(2)}) collective-permute-start(bf16[4,16,384]{2,1,0:T(8,128)(2,1)} %get-tuple-element.22), channel_id=1, source_target_pairs={{0,96},{32,0},{64,32},{96,64},{1,97},{33,1},{65,33},{97,65},{2,98}... | collective-permute-start | bytes 147464 | tf_op jit(solution)/shard_map/ppermute | solution.py:318
  132.5 0.8 collective-permute-done.a1_ref
  133.3 0.8 collective-permute-done.1.a2_ref
  134.2 1.3 collective-permute-done.2.a3_ref
  135.4 0.0 copy-done.1
  135.5 0.6 copy-done.3
  136.1 1.6 %add_groups.1 = (f32[4,16,160]{2,1,0:T(8,128)}, f32[4,16,128]{2,1,0:T(8,128)}) custom-call(f32[4,16,384]{2,1,0:T(8,128)} %get-tuple-element.19.a0_ref, bf16[4,16,384]{2,1,0:T(8,128)(2,1)} %copy-done.1, bf16[4,16,384]{2,1,0:T(8,128)(2,1)} %copy-done.2, bf16[4,16,384]{2,1,0:T(8,128)(2,1)} %copy-done.3), custom_call_target="tpu_custom_call" | custom-call | tf_op jit(solution)/shard_map/add_groups/pallas_call | solution.py:277
  (10 shorter events, 0.1 us)
Async XLA Ops:
  4.6 41.5 %all-to-all-start.1 = ((bf16[128,16,512]{2,1,0:T(8,128)(2,1)}), bf16[128,16,512]{2,1,0:T(8,128)(2,1)S(1)}, u32[]{:S(2)}, u32[]{:S(2)}) async-start(bf16[128,16,512]{2,1,0:T(8,128)(2,1)} %gather_fusion.1), calls=%async_computation.1 | async-start | bytes 4194304 | tf_op jit(solution)/shard_map/all_to_all | solution.py:306
  17.7 34.2 %copy-start.4 = (bf16[1,256,16]{1,2,0:T(8,128)(2,1)S(1)}, bf16[1,256,16]{1,2,0:T(8,128)(2,1)}, u32[]{:S(2)}) copy-start(bf16[1,256,16]{1,2,0:T(8,128)(2,1)} %param.14) | copy-start | bytes 24580
  46.1 5.8 %copy-start = (bf16[128,16,512]{2,1,0:T(8,128)(2,1)}, bf16[128,16,512]{2,1,0:T(8,128)(2,1)S(1)}, u32[]{:S(2)}) copy-start(bf16[128,16,512]{2,1,0:T(8,128)(2,1)S(1)} %all-to-all-done.1) | copy-start | bytes 6291460
  46.1 35.8 %all-to-all-start = ((bf16[128,16,512]{2,1,0:T(8,128)(2,1)}), bf16[128,16,512]{2,1,0:T(8,128)(2,1)}, u32[]{:S(2)}, u32[]{:S(2)}) async-start(bf16[128,16,512]{2,1,0:T(8,128)(2,1)} %gather_fusion), calls=%async_computation | async-start | bytes 4194304 | tf_op jit(solution)/shard_map/all_to_all | solution.py:306
  127.3 6.0 %collective-permute-start = (bf16[4,16,384]{2,1,0:T(8,128)(2,1)}, bf16[4,16,384]{2,1,0:T(8,128)(2,1)S(1)}, u32[]{:S(2)}, u32[]{:S(2)}) collective-permute-start(bf16[4,16,384]{2,1,0:T(8,128)(2,1)} %get-tuple-element.20), channel_id=1, source_target_pairs={{0,32},{32,64},{64,96},{96,0},{1,33},{33,65},{65,97},{97,1},{2,34}... | collective-permute-start | bytes 147464 | tf_op jit(solution)/shard_map/ppermute | solution.py:318
  128.3 5.8 %collective-permute-start.1 = (bf16[4,16,384]{2,1,0:T(8,128)(2,1)}, bf16[4,16,384]{2,1,0:T(8,128)(2,1)S(1)}, u32[]{:S(2)}, u32[]{:S(2)}) collective-permute-start(bf16[4,16,384]{2,1,0:T(8,128)(2,1)} %get-tuple-element.21), channel_id=1, source_target_pairs={{0,64},{32,96},{64,0},{96,32},{1,65},{33,97},{65,1},{97,33},{2,66}... | collective-permute-start | bytes 147464 | tf_op jit(solution)/shard_map/ppermute | solution.py:318
  131.1 4.3 %collective-permute-start.2 = (bf16[4,16,384]{2,1,0:T(8,128)(2,1)}, bf16[4,16,384]{2,1,0:T(8,128)(2,1)S(1)}, u32[]{:S(2)}, u32[]{:S(2)}) collective-permute-start(bf16[4,16,384]{2,1,0:T(8,128)(2,1)} %get-tuple-element.22), channel_id=1, source_target_pairs={{0,96},{32,0},{64,32},{96,64},{1,97},{33,1},{65,33},{97,65},{2,98}... | collective-permute-start | bytes 147464 | tf_op jit(solution)/shard_map/ppermute | solution.py:318
  133.3 2.1 %copy-start.1 = (bf16[4,16,384]{2,1,0:T(8,128)(2,1)}, bf16[4,16,384]{2,1,0:T(8,128)(2,1)S(1)}, u32[]{:S(2)}) copy-start(bf16[4,16,384]{2,1,0:T(8,128)(2,1)S(1)} %collective-permute-done.a1_ref) | copy-start | bytes 147460
  134.2 1.3 copy-start.2
  135.4 0.6 copy-start.3
